TPU v7x, 32 devices: a whole 2x2x4 slice. The times are simulated.
32 devices in a mesh: groups: 2 (over y), space: 16 (over z, x, core).
Axes of the slice: x: 2, y: 2, z: 4, core: 2. Of those that a mesh axis runs over, the one named last changes fastest.
Arguments:
- image_latent: float32 [128, 16, 320], P(('groups', 'space')), parts along dimension 0, may hold values from -6 to 6
- kernel_first: float32 [3, 3, 320, 320], replicated, may hold values from -0.109375 to 0.109375
- bias_first: float32 [320], replicated, may hold values from -3 to 3
- kernel_second: float32 [3, 3, 320, 320], replicated, may hold values from -0.109375 to 0.109375
- bias_second: float32 [320], replicated, may hold values from -3 to 3
- patch_kernel: float32 [5120, 1280], P('space'), may hold values from -0.078125 to 0.078125
- patch_bias: float32 [1280], replicated, may hold values from -3 to 3
- coarse_first: float32 [3, 3, 1280, 1280], P(None, None, None, 'space'), may hold values from -0.0546875 to 0.0546875
- coarse_bias_first: float32 [1280], P('space'), may hold values from -3 to 3
- coarse_second: float32 [3, 3, 1280, 1280], P(None, None, 'space'), may hold values from -0.0546875 to 0.0546875
- coarse_bias_second: float32 [1280], replicated, may hold values from -3 to 3
Outputs:
- fine_result: float32 [128, 16, 320], P(('groups', 'space')), parts along dimension 0
- coarse_result: float32 [32, 4, 1280], P(('groups', 'space')), parts along dimension 0
There are 2 independent parts, one for each index of `groups`. A program takes and returns all parts, laid end to end along the dimension named above; an argument that names none is the same for every part. Nothing has to cross between parts.
All inputs are finite; a program needn't handle non-finite values.
Results may differ from a plain program's by a relative error of at most 0.000061.
Values sent between devices are 32-bit elements; how exact they have to be, the bound alone decides.
A program may use at most 128 MiB of HBM per device.

v0:
```python
import functools

import jax
import jax.numpy as jnp
from jax import lax
from jax.experimental import pallas as pl
from jax.experimental.pallas import tpu as pltpu
from jax.sharding import PartitionSpec as P

MESH = pl.DeviceIdType.MESH
F32 = jnp.float32
BF16 = jnp.bfloat16
EDGE = 8


def split(value):
    high = value.astype(BF16)
    return high, (value - high.astype(F32)).astype(BF16)


def silu(value):
    return value / (1.0 + jnp.exp(-value))


def mul(a, b):
    return jnp.dot(a, b, preferred_element_type=F32)


def window(ref, first, rows, width, dx):
    value = ref[pl.ds(first + dx - 1, rows), :]
    if dx != 1:
        column = lax.broadcasted_iota(jnp.int32, value.shape, 0) % width
        value = jnp.where(column == (0 if dx == 0 else width - 1), 0.0, value)
    return value


def stacked(ref, first, rows, width, dx):
    high, low = split(window(ref, first, rows, width, dx))
    return jnp.concatenate([high, low], axis=0)


def kernel(
    count,
    image, bias_first, bias_second, patch_bias, coarse_bias_first, coarse_bias_second,
    w1_hbm, w2_hbm, wp_hbm, w3_hbm, w4_hbm,
    fine_out, coarse_out,
    w1, w2, wp, w3, w4,
    w1h, w1l, wph, wpl, w3s, w4h, w4l,
    halo, pad1, pad2, fine, patch_out, patch_in, sum_out, sum_in, mine, gathered, pad3, pad4, last_out, last_in,
    load_sem, halo_send, halo_recv, send_sem, recv_sem,
):
    me = lax.axis_index("space")
    rows, width, channels = image.shape
    local = mine.shape[0]
    pixels = local * count
    outer = wp.shape[1]
    feature = wp.shape[0]
    part = w3.shape[2]
    gap = w3s.shape[2] // 2

    loads = [
        pltpu.make_async_copy(src, dst, load_sem.at[i])
        for i, (src, dst) in enumerate(((w1_hbm, w1), (w2_hbm, w2), (wp_hbm, wp), (w3_hbm, w3), (w4_hbm, w4)))
    ]
    for load in loads:
        load.start()

    barrier = pltpu.get_barrier_semaphore()

    def greet(off, carry):
        pl.semaphore_signal(barrier, inc=1, device_id={"space": lax.rem(me + off, count)}, device_id_type=MESH)
        return carry

    lax.fori_loop(1, count, greet, 0)
    pl.semaphore_wait(barrier, count - 1)

    def up_copy():
        return pltpu.make_async_remote_copy(
            src_ref=image.at[pl.ds(0, 2)], dst_ref=halo.at[1],
            send_sem=halo_send.at[0], recv_sem=halo_recv.at[1],
            device_id={"space": jnp.maximum(me - 1, 0)}, device_id_type=MESH)

    def down_copy():
        return pltpu.make_async_remote_copy(
            src_ref=image.at[pl.ds(rows - 2, 2)], dst_ref=halo.at[0],
            send_sem=halo_send.at[1], recv_sem=halo_recv.at[0],
            device_id={"space": jnp.minimum(me + 1, count - 1)}, device_id_type=MESH)

    @pl.when(me > 0)
    def _():
        up_copy().start()

    @pl.when(me < count - 1)
    def _():
        down_copy().start()

    @pl.when(me == 0)
    def _():
        halo[0] = jnp.zeros(halo.shape[1:], F32)

    @pl.when(me == count - 1)
    def _():
        halo[1] = jnp.zeros(halo.shape[1:], F32)

    total = (rows + 4) * width
    inner = rows * width
    edge = 2 * width
    zero1 = jnp.zeros((EDGE, channels), F32)
    pad1[pl.ds(0, EDGE), :] = zero1
    pad1[pl.ds(EDGE + total, EDGE), :] = zero1
    held = image[...].reshape(inner, channels)
    pad1[pl.ds(EDGE + edge, inner), :] = silu(held)
    pad2[pl.ds(0, EDGE), :] = zero1
    pad2[pl.ds(EDGE + total - edge, EDGE), :] = zero1
    zero3 = jnp.zeros((EDGE, outer), F32)
    pad3[pl.ds(0, EDGE), :] = zero3
    pad3[pl.ds(EDGE + pixels, EDGE), :] = zero3
    zero4 = jnp.zeros((EDGE, part), F32)
    pad4[pl.ds(0, EDGE), :] = zero4
    pad4[pl.ds(EDGE + pixels, EDGE), :] = zero4

    loads[0].wait()

    def split_first(t, carry):
        w1h[t], w1l[t] = split(w1[t])
        return carry

    lax.fori_loop(0, 9, split_first, 0)

    @pl.when(me > 0)
    def _():
        down_copy().wait_recv()

    @pl.when(me < count - 1)
    def _():
        up_copy().wait_recv()

    pad1[pl.ds(EDGE, edge), :] = silu(halo[0].reshape(edge, channels))
    pad1[pl.ds(EDGE + edge + inner, edge), :] = silu(halo[1].reshape(edge, channels))

    span = (rows + 2) * width
    acc = jnp.zeros((span, channels), F32)
    for dy in range(3):
        for dx in range(3):
            x = stacked(pad1, EDGE + dy * width, span, width, dx)
            both = mul(x, w1h[3 * dy + dx])
            acc = acc + (both[:span] + both[span:] + mul(x[:span], w1l[3 * dy + dx]))
    pad2[pl.ds(EDGE, span), :] = silu(acc + bias_first[...])

    @pl.when(me == 0)
    def _():
        pad2[pl.ds(EDGE, width), :] = jnp.zeros((width, channels), F32)

    @pl.when(me == count - 1)
    def _():
        pad2[pl.ds(EDGE + span - width, width), :] = jnp.zeros((width, channels), F32)

    loads[1].wait()
    acc = jnp.zeros((inner, channels), F32)
    for dy in range(3):
        for dx in range(3):
            x = stacked(pad2, EDGE + dy * width, inner, width, dx)
            wh, wl = split(w2[3 * dy + dx])
            both = mul(x, wh)
            acc = acc + (both[:inner] + both[inner:] + mul(x[:inner], wl))
    result = image[...].reshape(inner, channels) + (acc + bias_second[...])
    fine[...] = result
    fine_out[...] = result.reshape(rows, width, channels)

    per_row = width // 4
    for e in range(count):
        at = e * feature
        cell, channel = at // channels, at % channels
        ky, kx = cell // 4, cell % 4
        for p in range(local):
            row = (4 * (p // per_row) + ky) * width + 4 * (p % per_row) + kx
            patch_out[e, pl.ds(p, 1), :] = fine[pl.ds(row, 1), pl.ds(channel, feature)]

    def send_all(out, into, stage):
        def one(off, carry):
            peer = lax.rem(me + off, count)
            pltpu.make_async_remote_copy(
                src_ref=out(peer), dst_ref=into.at[me],
                send_sem=send_sem.at[stage], recv_sem=recv_sem.at[stage],
                device_id={"space": peer}, device_id_type=MESH).start()
            return carry

        lax.fori_loop(1, count, one, 0)

    def wait_all(into, sem):
        other = into.at[pl.ds(0, count - 1)]
        pltpu.make_async_copy(other, other, sem).wait()

    send_all(lambda peer: patch_out.at[peer], patch_in, 0)
    loads[2].wait()
    wph[...], wpl[...] = split(wp[...])
    patch_in[me] = patch_out[me]
    wait_all(patch_in, recv_sem.at[0])

    features = jnp.concatenate([patch_in[d] for d in range(count)], axis=0)
    high, low = split(features)
    x = jnp.concatenate([high, low], axis=0)
    chunk = 256
    for n in range(0, outer, chunk):
        cols = pl.ds(n, chunk)
        both = mul(x, wph[:, cols])
        value = both[:pixels] + both[pixels:] + mul(high, wpl[:, cols])
        for e in range(count):
            sum_out[e, :, cols] = value[local * e : local * (e + 1)]
    send_all(lambda peer: sum_out.at[peer], sum_in, 1)
    loads[3].wait()

    def split_third(t, carry):
        high, low = split(w3[t])
        w3s[t, :, pl.ds(0, part)] = high
        w3s[t, :, pl.ds(gap, part)] = low
        return carry

    lax.fori_loop(0, 9, split_third, 0)
    sum_in[me] = sum_out[me]
    wait_all(sum_in, recv_sem.at[1])

    def add_up(ref):
        value = ref[0]
        for d in range(1, count):
            value = value + ref[d]
        return value

    coarse_input = add_up(sum_in) + patch_bias[...]
    coarse_out[...] = coarse_input.reshape(coarse_out.shape)
    mine[...] = silu(coarse_input)
    send_all(lambda peer: mine, gathered, 2)
    loads[4].wait()

    def split_fourth(t, carry):
        w4h[t], w4l[t] = split(w4[t])
        return carry

    lax.fori_loop(0, 9, split_fourth, 0)
    gathered[me] = mine[...]
    wait_all(gathered, recv_sem.at[2])
    for d in range(count):
        pad3[pl.ds(EDGE + local * d, local), :] = gathered[d]

    acc = jnp.zeros((2 * pixels, 2 * gap), F32)
    for dy in range(3):
        for dx in range(3):
            x = stacked(pad3, EDGE + (dy - 1) * per_row, pixels, per_row, dx)
            acc = acc + mul(x, w3s[3 * dy + dx])
    third = acc[:pixels, :part] + acc[:pixels, gap : gap + part] + acc[pixels:, :part]
    pad4[pl.ds(EDGE, pixels), :] = silu(third + coarse_bias_first[...])

    taps = [
        stacked(pad4, EDGE + (dy - 1) * per_row, pixels, per_row, dx)
        for dy in range(3) for dx in range(3)
    ]
    for n in range(0, outer, chunk):
        cols = pl.ds(n, chunk)
        both = jnp.zeros((2 * pixels, chunk), F32)
        value = jnp.zeros((pixels, chunk), F32)
        for t in range(9):
            both = both + mul(taps[t], w4h[t, :, cols])
            value = value + mul(taps[t][:pixels], w4l[t, :, cols])
        value = value + both[:pixels] + both[pixels:]
        for e in range(count):
            last_out[e, :, cols] = value[local * e : local * (e + 1)]
    send_all(lambda peer: last_out.at[peer], last_in, 3)
    last_in[me] = last_out[me]
    wait_all(last_in, recv_sem.at[3])
    fourth = add_up(last_in) + coarse_bias_second[...]
    coarse_out[...] = coarse_out[...] + fourth.reshape(coarse_out.shape)

    @pl.when(me > 0)
    def _():
        up_copy().wait_send()

    @pl.when(me < count - 1)
    def _():
        down_copy().wait_send()

    wait_all(patch_in, send_sem.at[0])
    wait_all(sum_in, send_sem.at[1])
    wait_all(gathered, send_sem.at[2])
    wait_all(last_in, send_sem.at[3])


def body(
    image_latent,
    kernel_first,
    bias_first,
    kernel_second,
    bias_second,
    patch_kernel,
    patch_bias,
    coarse_first,
    coarse_bias_first,
    coarse_second,
    coarse_bias_second,
):
    count = lax.axis_size("space")
    rows, width, channels = image_latent.shape
    feature, outer = patch_kernel.shape
    part = coarse_first.shape[3]
    local = (rows // 4) * (width // 4)
    pixels = local * count
    gap = -(-part // 128) * 128
    total = (rows + 4) * width
    vmem = pl.BlockSpec(memory_space=pltpu.VMEM)
    hbm = pl.BlockSpec(memory_space=pl.ANY)
    dma = pltpu.SemaphoreType.DMA
    weights = (
        kernel_first.reshape(9, channels, channels),
        kernel_second.reshape(9, channels, channels),
        patch_kernel,
        coarse_first.reshape(9, outer, part),
        coarse_second.reshape(9, part, outer),
    )
    slots = (count, local, outer)
    return pl.pallas_call(
        functools.partial(kernel, count),
        out_shape=(
            jax.ShapeDtypeStruct(image_latent.shape, F32),
            jax.ShapeDtypeStruct((rows // 4, width // 4, outer), F32),
        ),
        in_specs=[vmem] * 6 + [hbm] * 5,
        out_specs=(vmem, vmem),
        scratch_shapes=[pltpu.VMEM(w.shape, F32) for w in weights]
        + [
            pltpu.VMEM((9, channels, channels), BF16),
            pltpu.VMEM((9, channels, channels), BF16),
            pltpu.VMEM((feature, outer), BF16),
            pltpu.VMEM((feature, outer), BF16),
            pltpu.VMEM((9, outer, 2 * gap), BF16),
            pltpu.VMEM((9, part, outer), BF16),
            pltpu.VMEM((9, part, outer), BF16),
            pltpu.VMEM((2, 2, width, channels), F32),
            pltpu.VMEM((total + 2 * EDGE, channels), F32),
            pltpu.VMEM((total - 2 * width + 2 * EDGE, channels), F32),
            pltpu.VMEM((rows * width, channels), F32),
            pltpu.VMEM((count, local, feature), F32),
            pltpu.VMEM((count, local, feature), F32),
            pltpu.VMEM(slots, F32),
            pltpu.VMEM(slots, F32),
            pltpu.VMEM((local, outer), F32),
            pltpu.VMEM(slots, F32),
            pltpu.VMEM((pixels + 2 * EDGE, outer), F32),
            pltpu.VMEM((pixels + 2 * EDGE, part), F32),
            pltpu.VMEM(slots, F32),
            pltpu.VMEM(slots, F32),
            dma((5,)),
            dma((2,)),
            dma((2,)),
            dma((4,)),
            dma((4,)),
        ],
        compiler_params=pltpu.CompilerParams(
            collective_id=0, has_side_effects=True, vmem_limit_bytes=60 * 1024 * 1024
        ),
    )(
        image_latent,
        bias_first[None],
        bias_second[None],
        patch_bias[None],
        coarse_bias_first[None],
        coarse_bias_second[None],
        *weights,
    )


def solution(mesh):
    placed = (
        P(("groups", "space"), None, None),
        P(),
        P(),
        P(),
        P(),
        P("space", None),
        P(),
        P(None, None, None, "space"),
        P("space"),
        P(None, None, "space", None),
        P(),
    )
    return jax.shard_map(
        body,
        mesh=mesh,
        in_specs=placed,
        out_specs=(P(("groups", "space"), None, None), P(("groups", "space"), None, None)),
        check_vma=False,
    )
```

profile of v0, /device:TPU:0, one launch (start us, length us, event | category | flops | bytes accessed | tf_op | source)
XLA Modules:
  0.0 60.0 jit_solution(7374639355606102049)
XLA Ops:
  0.6 1.3 %broadcast_in_dim.15.bias_first = f32[1,320]{1,0:T(1,128)} reshape(f32[320]{0:T(512)} %param.13) | data formatting | bytes 2560 | tf_op jit(solution)/shard_map/broadcast_in_dim | solution.py:361
  1.9 1.3 %broadcast_in_dim.16.bias_second = f32[1,320]{1,0:T(1,128)} reshape(f32[320]{0:T(512)} %param.15) | data formatting | bytes 2560 | tf_op jit(solution)/shard_map/broadcast_in_dim | solution.py:362
  3.2 1.3 %broadcast_in_dim.17.patch_bias = f32[1,1280]{1,0:T(1,128)} reshape(f32[1280]{0:T(1024)} %param.17) | data formatting | bytes 10240 | tf_op jit(solution)/shard_map/broadcast_in_dim | solution.py:363
  4.5 1.3 %broadcast_in_dim.19.coarse_bias_second = f32[1,1280]{1,0:T(1,128)} reshape(f32[1280]{0:T(1024)} %param.21) | data formatting | bytes 10240 | tf_op jit(solution)/shard_map/broadcast_in_dim | solution.py:365
  5.7 5.9 %copy.13 = f32[3,3,1280,80]{3,2,1,0:T(8,128)} copy(f32[3,3,1280,80]{2,3,1,0:T(8,128)} %param.18) | data formatting | bytes 7372800 | tf_op args[7]
  11.6 45.5 %shard_map.122 = (f32[4,16,320]{2,1,0:T(8,128)}, f32[1,4,1280]{2,1,0:T(4,128)}) custom-call(f32[4,16,320]{2,1,0:T(8,128)} %image.1, f32[1,320]{1,0:T(1,128)} %broadcast_in_dim.15.bias_first, f32[1,320]{1,0:T(1,128)} %broadcast_in_dim.16.bias_second, f32[1,1280]{1,0:T(1,128)} %broadcast_in_dim.17.patch_bias, f32[1,80]{1,0:T(1,128)} %bitcast.9, ...), custom_call_target="tpu_custom_call" | custom-call | tf_op jit(solution)/shard_map/pallas_call | solution.py:319
  57.1 1.5 %copy.16 = f32[4,16,320]{2,1,0:T(8,128)} copy(f32[4,16,320]{2,1,0:T(8,128)} %get-tuple-element.4) | data formatting | bytes 163840
  58.7 1.3 %copy.17 = f32[1,4,1280]{2,1,0:T(4,128)} copy(f32[1,4,1280]{2,1,0:T(4,128)} %get-tuple-element.5) | data formatting | bytes 40960
where the time goes:
time: 61.1 us; the launch traced here: 60 us
  Pallas kernels  45.5 us (74%)
  local copies, waits for them, and re-layouts  13.8 us (23%)
  between operations  0.64 us (1%)
    pallas_call x1, Pallas kernels, body(): pl.pallas_call(functools.partial(kernel, count), out_shape=(jax.ShapeDtyp...  45.5 us
    unnamed x3, local copies, waits for them, and re-layouts  8.73 us
    broadcast_in_dim x1, local copies, waits for them, and re-layouts, body(): patch_bias[None]  1.29 us
    broadcast_in_dim x1, local copies, waits for them, and re-layouts, body(): coarse_bias_second[None]  1.29 us
    broadcast_in_dim x1, local copies, waits for them, and re-layouts, body(): bias_second[None]  1.27 us
    broadcast_in_dim x1, local copies, waits for them, and re-layouts, body(): bias_first[None]  1.26 us

commit v1 on v0

--- a/solution.py
+++ b/solution.py
@@ -24,6 +24,10 @@
 
 def mul(a, b):
     return jnp.dot(a, b, preferred_element_type=F32)
+
+
+def mul_rows(a, b):
+    return lax.dot_general(a, b, (((1,), (1,)), ((), ())), preferred_element_type=F32)
 
 
 def window(ref, first, rows, width, dx):
@@ -55,8 +59,8 @@
     pixels = local * count
     outer = wp.shape[1]
     feature = wp.shape[0]
-    part = w3.shape[2]
-    gap = w3s.shape[2] // 2
+    part = w3.shape[1]
+    gap = w3s.shape[1] // 2
 
     loads = [
         pltpu.make_async_copy(src, dst, load_sem.at[i])
@@ -212,8 +216,8 @@
 
     def split_third(t, carry):
         high, low = split(w3[t])
-        w3s[t, :, pl.ds(0, part)] = high
-        w3s[t, :, pl.ds(gap, part)] = low
+        w3s[t, pl.ds(0, part), :] = high
+        w3s[t, pl.ds(gap, part), :] = low
         return carry
 
     lax.fori_loop(0, 9, split_third, 0)
@@ -246,7 +250,7 @@
     for dy in range(3):
         for dx in range(3):
             x = stacked(pad3, EDGE + (dy - 1) * per_row, pixels, per_row, dx)
-            acc = acc + mul(x, w3s[3 * dy + dx])
+            acc = acc + mul_rows(x, w3s[3 * dy + dx])
     third = acc[:pixels, :part] + acc[:pixels, gap : gap + part] + acc[pixels:, :part]
     pad4[pl.ds(EDGE, pixels), :] = silu(third + coarse_bias_first[...])
 
@@ -303,7 +307,7 @@
     part = coarse_first.shape[3]
     local = (rows // 4) * (width // 4)
     pixels = local * count
-    gap = -(-part // 128) * 128
+    gap = -(-part // 16) * 16
     total = (rows + 4) * width
     vmem = pl.BlockSpec(memory_space=pltpu.VMEM)
     hbm = pl.BlockSpec(memory_space=pl.ANY)
@@ -312,7 +316,7 @@
         kernel_first.reshape(9, channels, channels),
         kernel_second.reshape(9, channels, channels),
         patch_kernel,
-        coarse_first.reshape(9, outer, part),
+        jnp.swapaxes(coarse_first, 2, 3).reshape(9, part, outer),
         coarse_second.reshape(9, part, outer),
     )
     slots = (count, local, outer)
@@ -330,7 +334,7 @@
             pltpu.VMEM((9, channels, channels), BF16),
             pltpu.VMEM((feature, outer), BF16),
             pltpu.VMEM((feature, outer), BF16),
-            pltpu.VMEM((9, outer, 2 * gap), BF16),
+            pltpu.VMEM((9, 2 * gap, outer), BF16),
             pltpu.VMEM((9, part, outer), BF16),
             pltpu.VMEM((9, part, outer), BF16),
             pltpu.VMEM((2, 2, width, channels), F32),

time: 61.1 us -> 55.4 us (0.907)
  local copies, waits for them, and re-layouts: 13.8 us -> 7.97 us
    unnamed x3 -> x2, local copies, waits for them, and re-layouts: 8.73 us -> 2.87 us
where the time goes in v1:
time: 55.4 us; the launch traced here: 54.4 us
  Pallas kernels  45.8 us (83%)
  local copies, waits for them, and re-layouts  7.97 us (14%)
  between operations  0.64 us (1%)
    pallas_call x1, Pallas kernels, body(): pl.pallas_call(functools.partial(kernel, count), out_shape=(jax.ShapeDtyp...  45.8 us
    unnamed x2, local copies, waits for them, and re-layouts  2.87 us
    broadcast_in_dim x1, local copies, waits for them, and re-layouts, body(): patch_bias[None]  1.29 us
    broadcast_in_dim x1, local copies, waits for them, and re-layouts, body(): coarse_bias_second[None]  1.29 us
    broadcast_in_dim x1, local copies, waits for them, and re-layouts, body(): bias_first[None]  1.26 us
    broadcast_in_dim x1, local copies, waits for them, and re-layouts, body(): bias_second[None]  1.24 us

profile of v1, /device:TPU:0, one launch (start us, length us, event | category | flops | bytes accessed | tf_op | source)
XLA Modules:
  0.0 54.4 jit_solution(13566275613711588501)
XLA Ops:
  0.6 1.3 %broadcast_in_dim.15.bias_first = f32[1,320]{1,0:T(1,128)} reshape(f32[320]{0:T(512)} %param.13) | data formatting | bytes 2560 | tf_op jit(solution)/shard_map/broadcast_in_dim | solution.py:365
  1.9 1.2 %broadcast_in_dim.16.bias_second = f32[1,320]{1,0:T(1,128)} reshape(f32[320]{0:T(512)} %param.15) | data formatting | bytes 2560 | tf_op jit(solution)/shard_map/broadcast_in_dim | solution.py:366
  3.1 1.3 %broadcast_in_dim.17.patch_bias = f32[1,1280]{1,0:T(1,128)} reshape(f32[1280]{0:T(1024)} %param.17) | data formatting | bytes 10240 | tf_op jit(solution)/shard_map/broadcast_in_dim | solution.py:367
  4.4 1.3 %broadcast_in_dim.19.coarse_bias_second = f32[1,1280]{1,0:T(1,128)} reshape(f32[1280]{0:T(1024)} %param.21) | data formatting | bytes 10240 | tf_op jit(solution)/shard_map/broadcast_in_dim | solution.py:369
  5.7 45.8 %shard_map.122 = (f32[4,16,320]{2,1,0:T(8,128)}, f32[1,4,1280]{2,1,0:T(4,128)}) custom-call(f32[4,16,320]{2,1,0:T(8,128)} %image.1, f32[1,320]{1,0:T(1,128)} %broadcast_in_dim.15.bias_first, f32[1,320]{1,0:T(1,128)} %broadcast_in_dim.16.bias_second, f32[1,1280]{1,0:T(1,128)} %broadcast_in_dim.17.patch_bias, f32[1,80]{1,0:T(1,128)} %bitcast.11, ...), custom_call_target="tpu_custom_call" | custom-call | tf_op jit(solution)/shard_map/pallas_call | solution.py:323
  51.5 1.5 %copy.15 = f32[4,16,320]{2,1,0:T(8,128)} copy(f32[4,16,320]{2,1,0:T(8,128)} %get-tuple-element.4) | data formatting | bytes 163840
  53.0 1.3 %copy.16 = f32[1,4,1280]{2,1,0:T(4,128)} copy(f32[1,4,1280]{2,1,0:T(4,128)} %get-tuple-element.5) | data formatting | bytes 40960

commit v2 on v1

--- a/solution.py
+++ b/solution.py
@@ -180,11 +180,11 @@
             row = (4 * (p // per_row) + ky) * width + 4 * (p % per_row) + kx
             patch_out[e, pl.ds(p, 1), :] = fine[pl.ds(row, 1), pl.ds(channel, feature)]
 
-    def send_all(out, into, stage):
+    def send_all(out, into, stage, base=0):
         def one(off, carry):
             peer = lax.rem(me + off, count)
             pltpu.make_async_remote_copy(
-                src_ref=out(peer), dst_ref=into.at[me],
+                src_ref=out(peer), dst_ref=into.at[base + me],
                 send_sem=send_sem.at[stage], recv_sem=recv_sem.at[stage],
                 device_id={"space": peer}, device_id_type=MESH).start()
             return carry
@@ -192,7 +192,7 @@
         lax.fori_loop(1, count, one, 0)
 
     def wait_all(into, sem):
-        other = into.at[pl.ds(0, count - 1)]
+        other = into.at[pl.ds(0, into.shape[0] // count * (count - 1))]
         pltpu.make_async_copy(other, other, sem).wait()
 
     send_all(lambda peer: patch_out.at[peer], patch_in, 0)
@@ -204,14 +204,15 @@
     features = jnp.concatenate([patch_in[d] for d in range(count)], axis=0)
     high, low = split(features)
     x = jnp.concatenate([high, low], axis=0)
-    chunk = 256
+    chunk = sum_out.shape[2]
     for n in range(0, outer, chunk):
         cols = pl.ds(n, chunk)
+        base = n // chunk * count
         both = mul(x, wph[:, cols])
         value = both[:pixels] + both[pixels:] + mul(high, wpl[:, cols])
         for e in range(count):
-            sum_out[e, :, cols] = value[local * e : local * (e + 1)]
-    send_all(lambda peer: sum_out.at[peer], sum_in, 1)
+            sum_out[base + e] = value[local * e : local * (e + 1)]
+        send_all(lambda peer: sum_out.at[base + peer], sum_in, 1, base)
     loads[3].wait()
 
     def split_third(t, carry):
@@ -221,14 +222,18 @@
         return carry
 
     lax.fori_loop(0, 9, split_third, 0)
-    sum_in[me] = sum_out[me]
+    for base in range(0, sum_in.shape[0], count):
+        sum_in[base + me] = sum_out[base + me]
     wait_all(sum_in, recv_sem.at[1])
 
     def add_up(ref):
-        value = ref[0]
-        for d in range(1, count):
-            value = value + ref[d]
-        return value
+        values = []
+        for base in range(0, ref.shape[0], count):
+            value = ref[base]
+            for d in range(1, count):
+                value = value + ref[base + d]
+            values.append(value)
+        return jnp.concatenate(values, axis=1)
 
     coarse_input = add_up(sum_in) + patch_bias[...]
     coarse_out[...] = coarse_input.reshape(coarse_out.shape)
@@ -260,6 +265,7 @@
     ]
     for n in range(0, outer, chunk):
         cols = pl.ds(n, chunk)
+        base = n // chunk * count
         both = jnp.zeros((2 * pixels, chunk), F32)
         value = jnp.zeros((pixels, chunk), F32)
         for t in range(9):
@@ -267,9 +273,9 @@
             value = value + mul(taps[t][:pixels], w4l[t, :, cols])
         value = value + both[:pixels] + both[pixels:]
         for e in range(count):
-            last_out[e, :, cols] = value[local * e : local * (e + 1)]
-    send_all(lambda peer: last_out.at[peer], last_in, 3)
-    last_in[me] = last_out[me]
+            last_out[base + e] = value[local * e : local * (e + 1)]
+        send_all(lambda peer: last_out.at[base + peer], last_in, 3, base)
+        last_in[base + me] = last_out[base + me]
     wait_all(last_in, recv_sem.at[3])
     fourth = add_up(last_in) + coarse_bias_second[...]
     coarse_out[...] = coarse_out[...] + fourth.reshape(coarse_out.shape)
@@ -320,6 +326,7 @@
         coarse_second.reshape(9, part, outer),
     )
     slots = (count, local, outer)
+    pieces = (outer // 256 * count, local, 256)
     return pl.pallas_call(
         functools.partial(kernel, count),
         out_shape=(
@@ -343,14 +350,14 @@
             pltpu.VMEM((rows * width, channels), F32),
             pltpu.VMEM((count, local, feature), F32),
             pltpu.VMEM((count, local, feature), F32),
-            pltpu.VMEM(slots, F32),
-            pltpu.VMEM(slots, F32),
+            pltpu.VMEM(pieces, F32),
+            pltpu.VMEM(pieces, F32),
             pltpu.VMEM((local, outer), F32),
             pltpu.VMEM(slots, F32),
             pltpu.VMEM((pixels + 2 * EDGE, outer), F32),
             pltpu.VMEM((pixels + 2 * EDGE, part), F32),
-            pltpu.VMEM(slots, F32),
-            pltpu.VMEM(slots, F32),
+            pltpu.VMEM(pieces, F32),
+            pltpu.VMEM(pieces, F32),
             dma((5,)),
             dma((2,)),
             dma((2,)),

time: 55.4 us -> 56.7 us (1.023); the launches traced: 54.4 us -> 56.4 us
  Pallas kernels: 45.8 us -> 47.7 us
    pallas_call x1, Pallas kernels: 45.8 us -> 47.7 us  [body(): pl.pallas_call(functools.partial(kernel, count), out_shape=(jax.ShapeDtyp...]
where the time goes in v2:
time: 56.7 us; the launch traced here: 56.4 us
  Pallas kernels  47.7 us (84%)
  local copies, waits for them, and re-layouts  7.97 us (14%)
  between operations  0.64 us (1%)
    pallas_call x1, Pallas kernels, body(): pl.pallas_call(functools.partial(kernel, count), out_shape=(jax.ShapeDtyp...  47.7 us
    unnamed x2, local copies, waits for them, and re-layouts  2.87 us
    broadcast_in_dim x1, local copies, waits for them, and re-layouts, body(): coarse_bias_second[None]  1.29 us
    broadcast_in_dim x1, local copies, waits for them, and re-layouts, body(): patch_bias[None]  1.29 us
    broadcast_in_dim x1, local copies, waits for them, and re-layouts, body(): bias_first[None]  1.26 us
    broadcast_in_dim x1, local copies, waits for them, and re-layouts, body(): bias_second[None]  1.24 us

profile of v2, /device:TPU:0, one launch (start us, length us, event | category | flops | bytes accessed | tf_op | source)
XLA Modules:
  0.0 56.4 jit_solution(17822620393819656544)
XLA Ops:
  0.6 1.3 %broadcast_in_dim.15.bias_first = f32[1,320]{1,0:T(1,128)} reshape(f32[320]{0:T(512)} %param.13) | data formatting | bytes 2560 | tf_op jit(solution)/shard_map/broadcast_in_dim | solution.py:372
  1.9 1.2 %broadcast_in_dim.16.bias_second = f32[1,320]{1,0:T(1,128)} reshape(f32[320]{0:T(512)} %param.15) | data formatting | bytes 2560 | tf_op jit(solution)/shard_map/broadcast_in_dim | solution.py:373
  3.1 1.3 %broadcast_in_dim.17.patch_bias = f32[1,1280]{1,0:T(1,128)} reshape(f32[1280]{0:T(1024)} %param.17) | data formatting | bytes 10240 | tf_op jit(solution)/shard_map/broadcast_in_dim | solution.py:374
  4.4 1.3 %broadcast_in_dim.19.coarse_bias_second = f32[1,1280]{1,0:T(1,128)} reshape(f32[1280]{0:T(1024)} %param.21) | data formatting | bytes 10240 | tf_op jit(solution)/shard_map/broadcast_in_dim | solution.py:376
  5.7 47.7 %shard_map.122 = (f32[4,16,320]{2,1,0:T(8,128)}, f32[1,4,1280]{2,1,0:T(4,128)}) custom-call(f32[4,16,320]{2,1,0:T(8,128)} %image.1, f32[1,320]{1,0:T(1,128)} %broadcast_in_dim.15.bias_first, f32[1,320]{1,0:T(1,128)} %broadcast_in_dim.16.bias_second, f32[1,1280]{1,0:T(1,128)} %broadcast_in_dim.17.patch_bias, f32[1,80]{1,0:T(1,128)} %bitcast.11, ...), custom_call_target="tpu_custom_call" | custom-call | tf_op jit(solution)/shard_map/pallas_call | solution.py:330
  53.5 1.5 %copy.15 = f32[4,16,320]{2,1,0:T(8,128)} copy(f32[4,16,320]{2,1,0:T(8,128)} %get-tuple-element.4) | data formatting | bytes 163840
  55.0 1.3 %copy.16 = f32[1,4,1280]{2,1,0:T(4,128)} copy(f32[1,4,1280]{2,1,0:T(4,128)} %get-tuple-element.5) | data formatting | bytes 40960
